TPU v7x, 32 devices: a whole 2x2x4 slice. The times are simulated.
32 devices in a mesh: ctx: 8 (over z, x), wsh: 4 (over y, core).
Axes of the slice: x: 2, y: 2, z: 4, core: 2. Of those that a mesh axis runs over, the one named last changes fastest.
Arguments:
- block_in: bfloat16 [4, 1024, 1088], P('wsh', 'ctx'), may hold values from -6 to 6
- doc_flags: int32 [4, 1024], P('wsh', 'ctx'), may hold values from 0 to 1, as said below
- ln1_gain: bfloat16 [1088], P('wsh'), may hold values from 0.5 to 1.5
- ln1_bias: bfloat16 [1088], P('wsh'), may hold values from -1 to 1
- w_qkv: bfloat16 [1088, 3264], P('wsh'), may hold values from -0.1875 to 0.1875
- qv_bias: bfloat16 [2176], P('wsh'), may hold values from -1 to 1
- w_out: bfloat16 [1088, 1088], P('wsh'), may hold values from -2 to 2
- out_bias: bfloat16 [1088], P('wsh'), may hold values from -1 to 1
- ln2_gain: bfloat16 [1088], P('wsh'), may hold values from 0.5 to 1.5
- ln2_bias: bfloat16 [1088], P('wsh'), may hold values from -1 to 1
- w_up: bfloat16 [1088, 4352], P(None, 'wsh'), may hold values from -0.1875 to 0.1875
- up_bias: bfloat16 [4352], P('wsh'), may hold values from -1 to 1
- w_down: bfloat16 [4352, 1088], P('wsh'), may hold values from -0.09375 to 0.09375
- down_bias: bfloat16 [1088], P('wsh'), may hold values from -1 to 1
- cotangent: bfloat16 [4, 1024, 1088], P('wsh', 'ctx'), may hold values from -6 to 6
Outputs:
- block_out: bfloat16 [4, 1024, 1088], P('wsh', 'ctx')
- input_grad: bfloat16 [4, 1024, 1088], P('wsh', 'ctx')
- grad_ln1_gain: float32 [1088], P('wsh')
- grad_ln1_bias: float32 [1088], P('wsh')
- grad_w_qkv: float32 [1088, 3264], P('wsh')
- grad_qv_bias: float32 [2176], P('wsh')
- grad_w_out: float32 [1088, 1088], P('wsh')
- grad_out_bias: float32 [1088], P('wsh')
- grad_ln2_gain: float32 [1088], P('wsh')
- grad_ln2_bias: float32 [1088], P('wsh')
- grad_w_up: float32 [1088, 4352], P(None, 'wsh')
- grad_up_bias: float32 [4352], P('wsh')
- grad_w_down: float32 [4352, 1088], P('wsh')
- grad_down_bias: float32 [1088], P('wsh')
- rms_values: float32 [4, 3], P('wsh')
Inputs may be any that keep to these rules, and one draw needn't show every extreme that they name: `doc_flags`: each stream has a 1 at position 0. In one stream, one document starts within the first 128 positions and ends within the last 128, and every other document of that stream lies inside those two ranges. In every other stream no document has more than 256 tokens, and one has exactly 256.
All inputs are finite; a program needn't handle non-finite values.
Results may differ from a plain program's by a relative error of at most 0.03.
Values may be sent and summed in bfloat16 or wider, within the bound.
No kernel may reach another device: no remote copies, remote signals or barrier semaphores. Data moves between devices by JAX's collectives and lax.ppermute only.
A program may use at most 448 MiB of HBM per device.

v0:
```python
import jax
import jax.numpy as jnp
from jax import lax
from jax.sharding import PartitionSpec as P

H = 17
HD = 64
EPSILON = 1e-05
NEGATIVE = -1e30


def prefix(shard, axis, combine, identity):
    size, mine = (lax.axis_size(axis), lax.axis_index(axis))
    everything = lax.all_gather(shard, axis)
    start = jnp.broadcast_to(jnp.asarray(identity, shard.dtype), shard.shape)

    def step(k, before):
        reached = k < mine
        new = combine(before, everything[k])
        return jnp.where(reached, new, before)

    return lax.fori_loop(0, size, step, start)


def normed(values, gain, shift):
    centre = values - jnp.mean(values, axis=-1, keepdims=True)
    spread = jnp.mean(centre * centre, axis=-1, keepdims=True)
    return centre * lax.rsqrt(spread + EPSILON) * gain + shift


def gelu_tanh(values):
    return jax.nn.gelu(values, approximate=True)


def add_counts(earlier, later):
    return earlier + later


def allowed_pairs(query_segment, query_place, key_segment, key_place):
    return (
        (query_segment[:, None] == key_segment[None, :])
        & (key_place[None, :] <= query_place[:, None])
    )[:, None, :]


def score_pairs(query_rows, key_rows, scaling):
    return (
        jnp.einsum("qhd,khd->qhk", query_rows, key_rows, preferred_element_type=jnp.float32)
        * scaling
    )


def contract_rows(left, right):
    return lax.dot_general(
        left, right, (((0,), (0,)), ((), ())), preferred_element_type=jnp.float32
    )


def contract_cols(left, right):
    return lax.dot_general(
        left, right, (((1,), (1,)), ((), ())), preferred_element_type=jnp.float32
    )


def local(
    block_in,
    doc_flags,
    ln1_gain,
    ln1_bias,
    w_qkv,
    qv_bias,
    w_out,
    out_bias,
    ln2_gain,
    ln2_bias,
    w_up,
    up_bias,
    w_down,
    down_bias,
    cotangent,
):
    tok_rows = block_in.shape[1]
    model_width = block_in.shape[2]
    scaling = HD ** (-0.5)
    ctx_count = lax.axis_size("ctx")
    running_count = jnp.cumsum(doc_flags[0])
    offset_count = prefix(running_count[-1], "ctx", add_counts, jnp.int32(0))
    local_segment = running_count + offset_count - 1
    local_place = lax.axis_index("ctx") * tok_rows + jnp.arange(tok_rows, dtype=jnp.int32)
    (
        gain_one,
        shift_one,
        qkv_full,
        qv_full,
        out_full,
        out_shift,
        gain_two,
        shift_two,
        up_full,
        up_shift,
        down_full,
        down_shift,
    ) = (
        lax.all_gather(ln1_gain, "wsh", axis=0, tiled=True),
        lax.all_gather(ln1_bias, "wsh", axis=0, tiled=True),
        lax.all_gather(w_qkv, "wsh", axis=0, tiled=True),
        lax.all_gather(qv_bias, "wsh", axis=0, tiled=True),
        lax.all_gather(w_out, "wsh", axis=0, tiled=True),
        lax.all_gather(out_bias, "wsh", axis=0, tiled=True),
        lax.all_gather(ln2_gain, "wsh", axis=0, tiled=True),
        lax.all_gather(ln2_bias, "wsh", axis=0, tiled=True),
        lax.all_gather(w_up, "wsh", axis=1, tiled=True),
        lax.all_gather(up_bias, "wsh", axis=0, tiled=True),
        lax.all_gather(w_down, "wsh", axis=0, tiled=True),
        lax.all_gather(down_bias, "wsh", axis=0, tiled=True),
    )
    gain_one, shift_one, gain_two, shift_two = [
        vector.astype(jnp.float32) for vector in (gain_one, shift_one, gain_two, shift_two)
    ]
    out_shift, up_shift, down_shift = [
        vector.astype(jnp.float32) for vector in (out_shift, up_shift, down_shift)
    ]
    input_rows = block_in[0].astype(jnp.float32)
    normed_one = normed(input_rows, gain_one, shift_one).astype(jnp.bfloat16)
    qkv_shift = jnp.concatenate(
        [qv_full[:model_width], jnp.zeros((model_width,), qv_full.dtype), qv_full[model_width:]]
    ).astype(jnp.float32)
    projected = (
        jnp.dot(normed_one, qkv_full, preferred_element_type=jnp.float32) + qkv_shift
    ).astype(jnp.bfloat16)
    queries = projected[:, :model_width].reshape(tok_rows, H, HD)
    key_rows = projected[:, model_width : 2 * model_width].reshape(tok_rows, H, HD)
    value_rows = projected[:, 2 * model_width :].reshape(tok_rows, H, HD)
    key_piece = lax.all_gather(key_rows, "ctx", axis=0, tiled=True)
    value_piece = lax.all_gather(value_rows, "ctx", axis=0, tiled=True)
    segment_piece = lax.all_gather(local_segment, "ctx", axis=0, tiled=True)
    piece_place = jnp.arange(key_piece.shape[0], dtype=jnp.int32)
    row_best = jnp.full((tok_rows, H), NEGATIVE, jnp.float32)
    score_block = score_pairs(queries, key_piece, scaling)
    allowed = allowed_pairs(local_segment, local_place, segment_piece, piece_place)
    new_best = jnp.maximum(row_best, jnp.max(jnp.where(allowed, score_block, NEGATIVE), axis=-1))
    weight_block = jnp.where(allowed, jnp.exp(score_block - new_best[..., None]), 0.0)
    row_total = jnp.sum(weight_block, axis=-1)
    weighted = jnp.einsum(
        "qhk,khd->qhd",
        weight_block.astype(jnp.bfloat16),
        value_piece,
        preferred_element_type=jnp.float32,
    )
    row_best, row_total, weighted = (new_best, row_total, weighted)
    log_total = row_best + jnp.log(row_total)
    attended = weighted / row_total[..., None]
    attended_low = attended.reshape(tok_rows, model_width).astype(jnp.bfloat16)
    attn_branch = jnp.dot(attended_low, out_full, preferred_element_type=jnp.float32) + out_shift
    residual = input_rows + attn_branch
    normed_two = normed(residual, gain_two, shift_two).astype(jnp.bfloat16)
    hidden_pre = jnp.dot(normed_two, up_full, preferred_element_type=jnp.float32) + up_shift
    hidden_act = gelu_tanh(hidden_pre).astype(jnp.bfloat16)
    mlp_sum = jnp.dot(hidden_act, down_full, preferred_element_type=jnp.float32)
    mlp_branch = mlp_sum + down_shift
    block_full = residual + mlp_branch
    square_sums = lax.psum(
        jnp.stack(
            [
                jnp.sum(attn_branch * attn_branch),
                jnp.sum(mlp_branch * mlp_branch),
                jnp.sum(block_full * block_full),
            ]
        ),
        "ctx",
    )
    rms_values = jnp.sqrt(square_sums / (tok_rows * ctx_count * model_width)).reshape(1, 3)
    out_grad = cotangent[0].astype(jnp.float32)
    mlp_grad = out_grad.astype(jnp.bfloat16)
    grad_down_shift = jnp.sum(mlp_grad.astype(jnp.float32), axis=0)
    grad_down = contract_rows(hidden_act, mlp_grad)
    act_grad = contract_cols(mlp_grad, down_full)
    unused_act, gelu_pull = jax.vjp(gelu_tanh, hidden_pre)
    pre_grad = gelu_pull(act_grad)[0].astype(jnp.bfloat16)
    grad_up_shift = jnp.sum(pre_grad.astype(jnp.float32), axis=0)
    grad_up = contract_rows(normed_two, pre_grad)
    normed_two_grad = contract_cols(pre_grad, up_full)
    unused_two, norm_two_pull = jax.vjp(normed, residual, gain_two, shift_two)
    residual_ln, grad_gain_two, grad_shift_two = norm_two_pull(normed_two_grad)
    residual_grad = out_grad + residual_ln
    attn_grad = residual_grad.astype(jnp.bfloat16)
    grad_out_shift = jnp.sum(attn_grad.astype(jnp.float32), axis=0)
    grad_out = contract_rows(attended_low, attn_grad)
    attended_grad = contract_cols(attn_grad, out_full).astype(jnp.bfloat16).reshape(tok_rows, H, HD)
    row_delta = jnp.sum(attended_grad.astype(jnp.float32) * attended, axis=-1)
    key_piece = lax.all_gather(key_rows, "ctx", axis=0, tiled=True)
    value_piece = lax.all_gather(value_rows, "ctx", axis=0, tiled=True)
    segment_piece = lax.all_gather(local_segment, "ctx", axis=0, tiled=True)
    piece_place = jnp.arange(key_piece.shape[0], dtype=jnp.int32)
    score_block = score_pairs(queries, key_piece, scaling)
    allowed = allowed_pairs(local_segment, local_place, segment_piece, piece_place)
    probability = jnp.where(allowed, jnp.exp(score_block - log_total[..., None]), 0.0)
    prob_grad = jnp.einsum(
        "qhd,khd->qhk", attended_grad, value_piece, preferred_element_type=jnp.float32
    )
    score_grad = (probability * (prob_grad - row_delta[..., None])).astype(jnp.bfloat16)
    query_grad = scaling * jnp.einsum(
        "qhk,khd->qhd", score_grad, key_piece, preferred_element_type=jnp.float32
    )
    query_piece = lax.all_gather(
        queries.astype(jnp.float32).astype(jnp.bfloat16), "ctx", axis=0, tiled=True
    ).astype(jnp.float32)
    grad_piece = lax.all_gather(
        attended_grad.astype(jnp.float32).astype(jnp.bfloat16), "ctx", axis=0, tiled=True
    )
    total_piece = lax.all_gather(log_total.astype(jnp.bfloat16), "ctx", axis=0, tiled=True).astype(
        jnp.float32
    )
    delta_piece = lax.all_gather(row_delta.astype(jnp.bfloat16), "ctx", axis=0, tiled=True).astype(
        jnp.float32
    )
    segment_piece = lax.all_gather(local_segment, "ctx", axis=0, tiled=True)
    query_low = query_piece.astype(jnp.bfloat16)
    piece_place = jnp.arange(query_piece.shape[0], dtype=jnp.int32)
    score_block = score_pairs(query_low, key_rows, scaling)
    allowed = allowed_pairs(segment_piece, piece_place, local_segment, local_place)
    probability = jnp.where(allowed, jnp.exp(score_block - total_piece[..., None]), 0.0)
    value_grad = jnp.einsum(
        "qhk,qhd->khd",
        probability.astype(jnp.bfloat16),
        grad_piece,
        preferred_element_type=jnp.float32,
    )
    prob_grad = jnp.einsum(
        "qhd,khd->qhk", grad_piece, value_rows, preferred_element_type=jnp.float32
    )
    score_grad = (probability * (prob_grad - delta_piece[..., None])).astype(jnp.bfloat16)
    key_grad = scaling * jnp.einsum(
        "qhk,qhd->khd", score_grad, query_low, preferred_element_type=jnp.float32
    )
    key_grad, value_grad = (key_grad, value_grad)
    qkv_grad = jnp.concatenate(
        [
            query_grad.reshape(tok_rows, model_width),
            key_grad.reshape(tok_rows, model_width),
            value_grad.reshape(tok_rows, model_width),
        ],
        axis=1,
    ).astype(jnp.bfloat16)
    qkv_grad_wide = qkv_grad.astype(jnp.float32)
    grad_qv_shift = jnp.concatenate(
        [
            jnp.sum(qkv_grad_wide[:, :model_width], axis=0),
            jnp.sum(qkv_grad_wide[:, 2 * model_width :], axis=0),
        ]
    )
    grad_qkv = contract_rows(normed_one, qkv_grad)
    normed_one_grad = contract_cols(qkv_grad, qkv_full)
    unused_one, norm_one_pull = jax.vjp(normed, input_rows, gain_one, shift_one)
    input_ln, grad_gain_one, grad_shift_one = norm_one_pull(normed_one_grad)
    input_grad = (residual_grad + input_ln).astype(jnp.bfloat16)
    (
        sum_gain_one,
        sum_shift_one,
        sum_qkv,
        sum_qv_shift,
        sum_out,
        sum_out_shift,
        sum_gain_two,
        sum_shift_two,
        sum_up,
        sum_up_shift,
        sum_down,
        sum_down_shift,
    ) = (
        lax.psum_scatter(
            grad_gain_one.astype(jnp.bfloat16), "wsh", scatter_dimension=0, tiled=True
        ).astype(jnp.float32),
        lax.psum_scatter(
            grad_shift_one.astype(jnp.bfloat16), "wsh", scatter_dimension=0, tiled=True
        ).astype(jnp.float32),
        lax.psum_scatter(
            grad_qkv.astype(jnp.bfloat16), "wsh", scatter_dimension=0, tiled=True
        ).astype(jnp.float32),
        lax.psum_scatter(
            grad_qv_shift.astype(jnp.bfloat16), "wsh", scatter_dimension=0, tiled=True
        ).astype(jnp.float32),
        lax.psum_scatter(
            grad_out.astype(jnp.bfloat16), "wsh", scatter_dimension=0, tiled=True
        ).astype(jnp.float32),
        lax.psum_scatter(
            grad_out_shift.astype(jnp.bfloat16), "wsh", scatter_dimension=0, tiled=True
        ).astype(jnp.float32),
        lax.psum_scatter(
            grad_gain_two.astype(jnp.bfloat16), "wsh", scatter_dimension=0, tiled=True
        ).astype(jnp.float32),
        lax.psum_scatter(
            grad_shift_two.astype(jnp.bfloat16), "wsh", scatter_dimension=0, tiled=True
        ).astype(jnp.float32),
        lax.psum_scatter(
            grad_up.astype(jnp.bfloat16), "wsh", scatter_dimension=1, tiled=True
        ).astype(jnp.float32),
        lax.psum_scatter(
            grad_up_shift.astype(jnp.bfloat16), "wsh", scatter_dimension=0, tiled=True
        ).astype(jnp.float32),
        lax.psum_scatter(
            grad_down.astype(jnp.bfloat16), "wsh", scatter_dimension=0, tiled=True
        ).astype(jnp.float32),
        lax.psum_scatter(
            grad_down_shift.astype(jnp.bfloat16), "wsh", scatter_dimension=0, tiled=True
        ).astype(jnp.float32),
    )
    totals = lax.psum(
        (
            sum_gain_one,
            sum_shift_one,
            sum_qkv,
            sum_qv_shift,
            sum_out,
            sum_out_shift,
            sum_gain_two,
            sum_shift_two,
            sum_up,
            sum_up_shift,
            sum_down,
            sum_down_shift,
        ),
        "ctx",
    )
    return (
        block_full.astype(jnp.bfloat16)[None],
        input_grad[None],
        totals[0],
        totals[1],
        totals[2],
        totals[3],
        totals[4],
        totals[5],
        totals[6],
        totals[7],
        totals[8],
        totals[9],
        totals[10],
        totals[11],
        rms_values,
    )


def solution(mesh):
    return jax.shard_map(
        local,
        mesh=mesh,
        in_specs=(
            P("wsh", "ctx", None),
            P("wsh", "ctx"),
            P("wsh"),
            P("wsh"),
            P("wsh", None),
            P("wsh"),
            P("wsh", None),
            P("wsh"),
            P("wsh"),
            P("wsh"),
            P(None, "wsh"),
            P("wsh"),
            P("wsh", None),
            P("wsh"),
            P("wsh", "ctx", None),
        ),
        out_specs=(
            P("wsh", "ctx", None),
            P("wsh", "ctx", None),
            P("wsh"),
            P("wsh"),
            P("wsh", None),
            P("wsh"),
            P("wsh", None),
            P("wsh"),
            P("wsh"),
            P("wsh"),
            P(None, "wsh"),
            P("wsh"),
            P("wsh", None),
            P("wsh"),
            P("wsh", None),
        ),
        check_vma=False,
    )
```

profile of v0, /device:TPU:0, one launch (start us, length us, event | category | flops | bytes accessed | tf_op | source)
XLA Modules:
  0.0 1312.7 jit_solution(13402227410424591593)
XLA Ops:
  18.2 14.6 %all-reduce.19 = (bf16[2176]{0:T(1024)(128)(2,1)S(1)}, bf16[1088]{0:T(1024)(128)(2,1)S(1)}, bf16[1088]{0:T(1024)(128)(2,1)S(1)}, bf16[1088]{0:T(1024)(128)(2,1)S...) all-reduce(bf16[2176]{0:T(1024)(128)(2,1)S(1)} %dynamic-update-slic, ...), channel_id=1, replica_groups=mesh['ctx'=8,'wsh'=4] {'wsh'}, use_global_device_ids=true, to_apply=%add.2 | all-reduce | flops 13056 | bytes 52224
  33.4 31.6 %all-gather.11.cloned.1.call-done = bf16[1088,3264]{1,0:T(8,128)(2,1)} async-done(((bf16[272,3264]{1,0:T(8,128)(2,1)}), bf16[1088,3264]{1,0:T(8,128)(2,1)}) %all-gather.11.cloned.1.call-update) | async-done | bytes 7102480 | tf_op jit(solution)/shard_map/all_gather | solution.py:106
  64.9 6.4 fusion.14
  80.3 11.5 all-reduce.3
  91.8 10.1 while.13
  102.0 32.7 %all-gather.1 = s32[1024,1]{1,0:T(8,128)S(1)} all-gather(s32[128,1]{1,0:T(8,128)S(1)} %get-tuple-element.154), channel_id=3, replica_groups=mesh['ctx'=8,'wsh'=4] {'ctx'}, dimensions={0}, use_global_device_ids=true | all-gather | bytes 4608 | tf_op jit(solution)/shard_map/all_gather | solution.py:136
  145.1 41.3 %all-gather.13.cloned.1.call-done = bf16[1024,17,64]{0,2,1:T(8,128)(2,1)} async-done(((bf16[128,17,64]{0,2,1:T(8,128)(2,1)}), bf16[1024,17,64]{0,2,1:T(8,128)(2,1)}) %all-gather.13.cloned.1.call-update) | async-done | bytes 2228240 | tf_op jit(solution)/shard_map/all_gather | solution.py:135
  186.3 6.8 fusion.107
  193.2 17.7 %all-gather.17.cloned.1.call-done = bf16[1088,1088]{1,0:T(8,128)(2,1)} async-done(((bf16[272,1088]{1,0:T(8,128)(2,1)}), bf16[1088,1088]{1,0:T(8,128)(2,1)}) %all-gather.17.cloned.1.call-update) | async-done | bytes 2367504 | tf_op jit(solution)/shard_map/all_gather | solution.py:108
  215.9 64.6 %all-gather.19.cloned.1.call-done = bf16[1088,4352]{0,1:T(8,128)(2,1)} async-done(((bf16[1088,1088]{0,1:T(8,128)(2,1)}), bf16[1088,4352]{0,1:T(8,128)(2,1)}) %all-gather.19.cloned.1.call-update) | async-done | bytes 9469968 | tf_op jit(solution)/shard_map/all_gather | solution.py:112
  280.5 7.2 convolution_add_fusion
  287.7 61.8 %all-gather.21.cloned.1.call-done = bf16[4352,1088]{1,0:T(8,128)(2,1)} async-done(((bf16[1088,1088]{1,0:T(8,128)(2,1)}), bf16[4352,1088]{1,0:T(8,128)(2,1)}) %all-gather.21.cloned.1.call-update) | async-done | bytes 9469968 | tf_op jit(solution)/shard_map/all_gather | solution.py:114
  349.5 7.8 fusion.108
  361.4 9.2 multiply_reduce_fusion.1
  379.2 26.6 %all_gather.81 = bf16[1024,17]{0,1:T(8,128)(2,1)S(1)} all-gather(bf16[128,17]{0,1:T(8,128)(2,1)S(1)} %get-tuple-element.147), channel_id=1, replica_groups=mesh['ctx'=8,'wsh'=4] {'ctx'}, dimensions={0}, use_global_device_ids=true | all-gather | bytes 39168 | tf_op jit(solution)/shard_map/all_gather | solution.py:211
  407.6 26.6 %all_gather.83 = bf16[1024,17]{0,1:T(8,128)(2,1)S(1)} all-gather(bf16[128,17]{0,1:T(8,128)(2,1)S(1)} %convert_element_type.201), channel_id=1, replica_groups=mesh['ctx'=8,'wsh'=4] {'ctx'}, dimensions={0}, use_global_device_ids=true | all-gather | bytes 39168 | tf_op jit(solution)/shard_map/all_gather | solution.py:214
  434.9 6.6 fusion.110
  441.5 9.5 fusion.47
  451.0 7.1 all-gather.25.cloned.1.call-done
  458.1 6.7 fusion.53
  464.8 10.5 fusion.50
  475.3 6.5 convolution_convert_fusion.2
  482.5 6.7 convolution_convert_fusion.1
  489.2 14.0 %copy.50 = bf16[1088,4352]{0,1:T(8,128)(2,1)} copy(bf16[1088,4352]{1,0:T(8,128)(2,1)} %convolution_convert_fusion.1) | data formatting | bytes 18939904
  503.3 6.3 convolution_convert_fusion
  514.5 5.3 fusion.96
  520.2 13.2 %all-reduce.18 = (bf16[1088]{0:T(1024)(128)(2,1)S(1)}, bf16[1088]{0:T(1024)(128)(2,1)S(1)}, bf16[2176]{0:T(1024)(128)(2,1)S(1)}, bf16[1088]{0:T(1024)(128)(2,1)S...) all-reduce(bf16[1088]{0:T(1024)(128)(2,1)S(1)} %get-tuple-element.9, ...), channel_id=4, replica_groups=mesh['ctx'=8,'wsh'=4] {'wsh'}, use_global_device_ids=true, to_apply=%region_15.16.clone | all-reduce | flops 13056 | bytes 52224
  534.8 26.8 %reduce-scatter.7.cloned.1.call-done = bf16[272,3264]{1,0:T(8,128)(2,1)} async-done(((bf16[1088,3264]{1,0:T(8,128)(2,1)}), bf16[272,3264]{1,0:T(8,128)(2,1)}) %reduce-scatter.7.cloned.1.call-update) | async-done | bytes 1775632 | tf_op jit(solution)/shard_map/reduce_scatter | solution.py:277
  561.6 84.9 %reduce-scatter.13.cloned.1.call-done = bf16[1088,1088]{1,0:T(8,128)(2,1)} async-done(((bf16[4352,1088]{1,0:T(8,128)(2,1)}), bf16[1088,1088]{1,0:T(8,128)(2,1)}) %reduce-scatter.13.cloned.1.call-update) | async-done | bytes 2367504
  646.5 4.1 copy.51
  650.7 80.6 %reduce-scatter.11.cloned.1.call-done = bf16[1088,1088]{1,0:T(8,128)(2,1)} async-done(((bf16[4352,1088]{1,0:T(8,128)(2,1)}), bf16[1088,1088]{1,0:T(8,128)(2,1)}) %reduce-scatter.11.cloned.1.call-update) | async-done | bytes 2367504 | tf_op jit(solution)/shard_map/reduce_scatter | solution.py:301
  731.3 573.8 %all-reduce.21 = (f32[272]{0:T(512)}, f32[272]{0:T(512)}, f32[272,3264]{1,0:T(8,128)}, f32[544]{0:T(1024)}, f32[272,1088]{1,0:T(8,128)}, /*index=5*/f32[272]{0:T...) all-reduce(f32[272]{0:T(512)S(1)} %get-tuple-element.176, ...), channel_id=1, replica_groups=mesh['ctx'=8,'wsh'=4] {'ctx'}, use_global_device_ids=true, to_apply=%region_16.17 | all-reduce | flops 3554499 | bytes 21333528 | tf_op jit(solution)/shard_map/psum | solution.py:308
  (198 shorter events, 59.3 us)
Async XLA Ops:
  7.2 25.8 %copy-start.2 = (bf16[1,128,1088]{1,2,0:T(8,128)(2,1)S(1)}, bf16[1,128,1088]{1,2,0:T(8,128)(2,1)}, u32[]{:S(2)}) copy-start(bf16[1,128,1088]{1,2,0:T(8,128)(2,1)} %param.17) | copy-start | bytes 835588
  7.2 57.8 %all-gather.11.cloned.1.call-start = ((), (), s32[]{:S(2)}) async-start(), calls=%async_computation.4 | async-start | bytes 9052160 | tf_op jit(solution)/shard_map/all_gather | solution.py:106
  7.9 128.1 %all-gather.15.cloned.1.call-start = ((), (), s32[]{:S(2)}) async-start(), calls=%async_computation.6 | async-start | bytes 2506752 | tf_op jit(solution)/shard_map/all_gather | solution.py:134
  33.2 38.2 %copy-start.17 = (f32[128]{0:T(128)}, f32[128]{0:T(128)S(1)}, u32[]{:S(2)}) copy-start(f32[128]{0:T(128)S(1)} %broadcast_multiply_fusion.1) | copy-start | bytes 1540
  33.3 38.0 %copy-start.37 = (f32[128]{0:T(128)}, f32[128]{0:T(128)S(1)}, u32[]{:S(2)}) copy-start(f32[128]{0:T(128)S(1)} %fusion.70) | copy-start | bytes 1540
  33.4 38.0 %copy-start.21 = (f32[128]{0:T(128)}, f32[128]{0:T(128)S(1)}, u32[]{:S(2)}) copy-start(f32[128]{0:T(128)S(1)} %fusion.82) | copy-start | bytes 1540
  72.3 114.0 %all-gather.13.cloned.1.call-start = ((), (), s32[]{:S(2)}) async-start(), calls=%async_computation.5 | async-start | bytes 2506752 | tf_op jit(solution)/shard_map/all_gather | solution.py:135
  73.1 137.8 %all-gather.17.cloned.1.call-start = ((), (), s32[]{:S(2)}) async-start(), calls=%async_computation.7 | async-start | bytes 3133440 | tf_op jit(solution)/shard_map/all_gather | solution.py:108
  73.7 206.8 %all-gather.19.cloned.1.call-start = ((), (), s32[]{:S(2)}) async-start(), calls=%async_computation.8 | async-start | bytes 12533760 | tf_op jit(solution)/shard_map/all_gather | solution.py:112
  77.0 59.1 %copy-start.7 = (bf16[128,1088]{0,1:T(8,128)(2,1)S(1)}, bf16[128,1088]{0,1:T(8,128)(2,1)}, u32[]{:S(2)}) copy-start(bf16[128,1088]{0,1:T(8,128)(2,1)} %get-tuple-element.156) | copy-start | bytes 835588
  77.0 272.6 %all-gather.21.cloned.1.call-start = ((), (), s32[]{:S(2)}) async-start(), calls=%async_computation.9 | async-start | bytes 12533760 | tf_op jit(solution)/shard_map/all_gather | solution.py:114
  77.5 357.4 %all-gather.23.cloned.1.call-start = ((), (), s32[]{:S(2)}) async-start(), calls=%async_computation.10 | async-start | bytes 2506752 | tf_op jit(solution)/shard_map/all_gather | solution.py:205
  102.0 34.0 %copy-start.28 = (s32[128]{0:T(128)}, s32[128]{0:T(128)S(1)}, u32[]{:S(2)}) copy-start(s32[128]{0:T(128)S(1)} %get-tuple-element.153) | copy-start | bytes 1540
  135.8 322.3 %all-gather.25.cloned.1.call-start = ((), (), s32[]{:S(2)}) async-start(), calls=%async_computation.11 | async-start | bytes 2506752 | tf_op jit(solution)/shard_map/all_gather | solution.py:208
  193.2 21.3 %copy-start.14 = (bf16[128,17,64]{0,2,1:T(8,128)(2,1)}, bf16[128,17,64]{0,2,1:T(8,128)(2,1)S(1)}, u32[]{:S(2)}) copy-start(bf16[128,17,64]{0,2,1:T(8,128)(2,1)S(1)} %get-tuple-element.166) | copy-start | bytes 835588
  215.9 133.7 %copy-start.6 = (bf16[1,128,1088]{1,2,0:T(8,128)(2,1)S(1)}, bf16[1,128,1088]{1,2,0:T(8,128)(2,1)}, u32[]{:S(2)}) copy-start(bf16[1,128,1088]{1,2,0:T(8,128)(2,1)} %param.31) | copy-start | bytes 835588
  349.5 7.8 copy-start
  361.4 9.2 copy-start.40
  374.3 160.5 %reduce-scatter.9.cloned.1.call-start = ((), (), s32[]{:S(2)}) async-start(), calls=%async_computation.13 | async-start | bytes 3133440 | tf_op jit(solution)/shard_map/reduce_scatter | solution.py:283
  377.7 183.9 %reduce-scatter.7.cloned.1.call-start = ((), (), s32[]{:S(2)}) async-start(), calls=%async_computation.12 | async-start | bytes 9052160 | tf_op jit(solution)/shard_map/reduce_scatter | solution.py:277
  434.9 6.6 copy-start.23
  451.0 13.8 %copy-start.16 = (pred[1024,128]{0,1:T(8,128)(4,1)S(1)}, pred[1024,128]{0,1:T(8,128)(4,1)}, u32[]{:S(2)}) copy-start(pred[1024,128]{0,1:T(8,128)(4,1)} %fusion.73) | copy-start | bytes 393220
  464.8 10.5 copy-start.18
  464.8 10.5 copy-start.22
  481.8 164.7 %reduce-scatter.13.cloned.1.call-start = ((), (), s32[]{:S(2)}) async-start(), calls=%async_computation.15 | async-start | bytes 12533760
  503.3 228.1 %reduce-scatter.11.cloned.1.call-start = ((), (), s32[]{:S(2)}) async-start(), calls=%async_computation.14 | async-start | bytes 12533760 | tf_op jit(solution)/shard_map/reduce_scatter | solution.py:301
  514.4 5.7 copy-start.24
  514.4 5.7 copy-start.30
  514.4 5.8 copy-start.31
  514.5 19.4 %copy-start.4 = (f32[128,1088]{0,1:T(8,128)S(1)}, f32[128,1088]{0,1:T(8,128)}, u32[]{:S(2)}) copy-start(f32[128,1088]{0,1:T(8,128)} %copy-done.3) | copy-start | bytes 1671172
  514.5 19.3 %copy-start.33 = (f32[128]{0:T(128)S(1)}, f32[128]{0:T(128)}, u32[]{:S(2)}) copy-start(f32[128]{0:T(128)} %copy-done.32) | copy-start | bytes 1540
  646.5 84.8 %copy-start.15 = (bf16[272,1088]{1,0:T(8,128)(2,1)S(1)}, bf16[272,1088]{1,0:T(8,128)(2,1)}, u32[]{:S(2)}) copy-start(bf16[272,1088]{1,0:T(8,128)(2,1)} %reduce-scatter.9.cloned.1.call-done) | copy-start | bytes 1775620
  (22 other events, 62.3 us)
Sparse Core Ops, SparseCore 0:
  9.6 55.3 all-gather.10
  72.5 60.5 all-gather.14
  135.1 51.2 all-gather.12
  187.7 23.0 all-gather.16
  212.9 67.5 all-gather.18
  281.9 67.5 all-gather.20
  352.1 53.1 all-gather.22
  407.4 50.6 all-gather.24
  461.2 32.1 reduce-scatter.8
  496.0 65.5 reduce-scatter.6
  564.2 82.2 reduce-scatter.12
  649.0 82.2 reduce-scatter.10
where the time goes:
time: 1320 us; the launch traced here: 1310 us
  blocking collectives  699 us (53%)
  waiting for transfers between devices  419 us (32%)
  matrix products  112 us (8%)
  local copies, waits for them, and re-layouts  44.5 us (3%)
  between operations  18.9 us (1%)
  other arithmetic  13.7 us (1%)
    psum x1, blocking collectives, local(): lax.psum((sum_gain_one, sum_shift_one, sum_qkv, sum_qv_shift, sum_out, su...  574 us
    unnamed x13, waiting for transfers between devices  87.5 us
    reduce_scatter x1, waiting for transfers between devices, local(): lax.psum_scatter(grad_down.astype(jnp.bfloat16), 'wsh', scatter_dimension...  80.6 us
    all_gather x1, waiting for transfers between devices, local(): lax.all_gather(w_up, 'wsh', axis=1, tiled=True)  64.6 us
    all_gather x1, waiting for transfers between devices, local(): lax.all_gather(w_down, 'wsh', axis=0, tiled=True)  61.8 us
    all_gather x1, waiting for transfers between devices, local(): value_piece = lax.all_gather(value_rows, 'ctx', axis=0, tiled=True)  41.3 us
    unnamed x108, local copies, waits for them, and re-layouts  38.1 us
    all_gather x1, blocking collectives, local(): segment_piece = lax.all_gather(local_segment, 'ctx', axis=0, tiled=True)  32.7 us
  transfers between devices with their start and end apart: 12, of which 9 were waited for; matrix products, arithmetic and copies ran while one was open for 12% of the time, Pallas kernels for 0%

commit v1 on v0

--- a/solution.py
+++ b/solution.py
@@ -133,7 +133,12 @@
     value_rows = projected[:, 2 * model_width :].reshape(tok_rows, H, HD)
     key_piece = lax.all_gather(key_rows, "ctx", axis=0, tiled=True)
     value_piece = lax.all_gather(value_rows, "ctx", axis=0, tiled=True)
-    segment_piece = lax.all_gather(local_segment, "ctx", axis=0, tiled=True)
+    ring = [local_segment]
+    for hop in range(7):
+        ring.append(lax.ppermute(ring[-1], "ctx", [(dev, (dev + 1) % 8) for dev in range(8)]))
+    segment_piece = jnp.roll(
+        jnp.concatenate(ring[::-1], axis=0), (lax.axis_index("ctx") + 1) * ring[0].shape[0], axis=0
+    )
     piece_place = jnp.arange(key_piece.shape[0], dtype=jnp.int32)
     row_best = jnp.full((tok_rows, H), NEGATIVE, jnp.float32)
     score_block = score_pairs(queries, key_piece, scaling)

time: 1320 us -> 1320 us (level)
    all_gather x1, waiting for transfers between devices: 41.3 us -> 0.02 us  [local(): value_piece = lax.all_gather(value_rows, 'ctx', axis=0, tiled=True)]
    ppermute x0 -> x7, waiting for transfers between devices: none -> 33.4 us  [local(): lax.ppermute(ring[-1], 'ctx', [(dev, (dev + 1) % 8) for dev in range(8)])]
    unnamed x108 -> x123, local copies, waits for them, and re-layouts: 38.1 us -> 38.2 us
  transfers between devices with their start and end apart: 12 -> 19, of which waited for: 9 -> 14; matrix products, arithmetic and copies ran while one was open for 12% -> 12% of each run, Pallas kernels for 0% -> 0%
where the time goes in v1:
time: 1320 us; the launch traced here: 1310 us
  blocking collectives  699 us (53%)
  waiting for transfers between devices  410 us (31%)
  matrix products  112 us (8%)
  local copies, waits for them, and re-layouts  44.7 us (3%)
  between operations  19 us (1%)
  other arithmetic  13.9 us (1%)
    psum x1, blocking collectives, local(): lax.psum((sum_gain_one, sum_shift_one, sum_qkv, sum_qv_shift, sum_out, su...  574 us
    unnamed x13, waiting for transfers between devices  87.5 us
    reduce_scatter x1, waiting for transfers between devices, local(): lax.psum_scatter(grad_down.astype(jnp.bfloat16), 'wsh', scatter_dimension...  80.6 us
    all_gather x1, waiting for transfers between devices, local(): lax.all_gather(w_up, 'wsh', axis=1, tiled=True)  64.6 us
    all_gather x1, waiting for transfers between devices, local(): lax.all_gather(w_down, 'wsh', axis=0, tiled=True)  61.8 us
    unnamed x123, local copies, waits for them, and re-layouts  38.2 us
    ppermute x7, waiting for transfers between devices, local(): lax.ppermute(ring[-1], 'ctx', [(dev, (dev + 1) % 8) for dev in range(8)])  33.4 us
    all_gather x1, blocking collectives, local(): segment_piece = lax.all_gather(local_segment, 'ctx', axis=0, tiled=True)  32.4 us
  transfers between devices with their start and end apart: 19, of which 14 were waited for; matrix products, arithmetic and copies ran while one was open for 12% of the time, Pallas kernels for 0%

profile of v1, /device:TPU:0, one launch (start us, length us, event | category | flops | bytes accessed | tf_op | source)
XLA Modules:
  0.0 1307.7 jit_solution(17301620748521152301)
XLA Ops:
  18.2 14.6 %all-reduce.19 = (bf16[2176]{0:T(1024)(128)(2,1)S(1)}, bf16[1088]{0:T(1024)(128)(2,1)S(1)}, bf16[1088]{0:T(1024)(128)(2,1)S(1)}, bf16[1088]{0:T(1024)(128)(2,1)S...) all-reduce(bf16[2176]{0:T(1024)(128)(2,1)S(1)} %dynamic-update-slic, ...), channel_id=1, replica_groups=mesh['ctx'=8,'wsh'=4] {'wsh'}, use_global_device_ids=true, to_apply=%add.2 | all-reduce | flops 13056 | bytes 52224
  33.4 31.6 %all-gather.11.cloned.1.call-done = bf16[1088,3264]{1,0:T(8,128)(2,1)} async-done(((bf16[272,3264]{1,0:T(8,128)(2,1)}), bf16[1088,3264]{1,0:T(8,128)(2,1)}) %all-gather.11.cloned.1.call-update) | async-done | bytes 7102480 | tf_op jit(solution)/shard_map/all_gather | solution.py:106
  64.9 6.4 fusion.14
  80.3 11.5 all-reduce.3
  91.8 10.1 while.13
  108.4 6.3 collective-permute-done.1
  114.7 6.3 collective-permute-done.2
  121.1 32.4 %all-gather.1 = s32[1024,1]{1,0:T(8,128)S(1)} all-gather(s32[128,1]{1,0:T(8,128)S(1)} %get-tuple-element.154), channel_id=3, replica_groups=mesh['ctx'=8,'wsh'=4] {'ctx'}, dimensions={0}, use_global_device_ids=true | all-gather | bytes 4608 | tf_op jit(solution)/shard_map/all_gather | solution.py:198
  159.9 6.0 collective-permute-done.5
  182.1 6.8 fusion.108
  189.0 17.0 %all-gather.17.cloned.1.call-done = bf16[1088,1088]{1,0:T(8,128)(2,1)} async-done(((bf16[272,1088]{1,0:T(8,128)(2,1)}), bf16[1088,1088]{1,0:T(8,128)(2,1)}) %all-gather.17.cloned.1.call-update) | async-done | bytes 2367504 | tf_op jit(solution)/shard_map/all_gather | solution.py:108
  211.0 64.6 %all-gather.19.cloned.1.call-done = bf16[1088,4352]{0,1:T(8,128)(2,1)} async-done(((bf16[1088,1088]{0,1:T(8,128)(2,1)}), bf16[1088,4352]{0,1:T(8,128)(2,1)}) %all-gather.19.cloned.1.call-update) | async-done | bytes 9469968 | tf_op jit(solution)/shard_map/all_gather | solution.py:112
  275.6 7.2 convolution_add_fusion
  282.8 61.8 %all-gather.21.cloned.1.call-done = bf16[4352,1088]{1,0:T(8,128)(2,1)} async-done(((bf16[1088,1088]{1,0:T(8,128)(2,1)}), bf16[4352,1088]{1,0:T(8,128)(2,1)}) %all-gather.21.cloned.1.call-update) | async-done | bytes 9469968 | tf_op jit(solution)/shard_map/all_gather | solution.py:114
  344.6 7.8 fusion.109
  356.5 9.2 multiply_reduce_fusion.1
  374.3 26.6 %all_gather.80 = bf16[1024,17]{0,1:T(8,128)(2,1)S(1)} all-gather(bf16[128,17]{0,1:T(8,128)(2,1)S(1)} %get-tuple-element.147), channel_id=1, replica_groups=mesh['ctx'=8,'wsh'=4] {'ctx'}, dimensions={0}, use_global_device_ids=true | all-gather | bytes 39168 | tf_op jit(solution)/shard_map/all_gather | solution.py:216
  402.8 26.6 %all_gather.82 = bf16[1024,17]{0,1:T(8,128)(2,1)S(1)} all-gather(bf16[128,17]{0,1:T(8,128)(2,1)S(1)} %convert_element_type.201), channel_id=1, replica_groups=mesh['ctx'=8,'wsh'=4] {'ctx'}, dimensions={0}, use_global_device_ids=true | all-gather | bytes 39168 | tf_op jit(solution)/shard_map/all_gather | solution.py:219
  430.0 6.6 fusion.111
  436.5 9.5 fusion.47
  446.0 7.1 all-gather.25.cloned.1.call-done
  453.1 6.7 fusion.53
  459.9 10.5 fusion.50
  470.4 6.5 convolution_convert_fusion.2
  477.6 6.7 convolution_convert_fusion.1
  484.3 14.0 %copy.50 = bf16[1088,4352]{0,1:T(8,128)(2,1)} copy(bf16[1088,4352]{1,0:T(8,128)(2,1)} %convolution_convert_fusion.1) | data formatting | bytes 18939904
  498.4 6.2 convolution_convert_fusion
  515.3 13.2 %all-reduce.18 = (bf16[1088]{0:T(1024)(128)(2,1)S(1)}, bf16[1088]{0:T(1024)(128)(2,1)S(1)}, bf16[2176]{0:T(1024)(128)(2,1)S(1)}, bf16[1088]{0:T(1024)(128)(2,1)S...) all-reduce(bf16[1088]{0:T(1024)(128)(2,1)S(1)} %get-tuple-element.9, ...), channel_id=4, replica_groups=mesh['ctx'=8,'wsh'=4] {'wsh'}, use_global_device_ids=true, to_apply=%region_15.16.clone | all-reduce | flops 13056 | bytes 52224
  529.9 26.8 %reduce-scatter.7.cloned.1.call-done = bf16[272,3264]{1,0:T(8,128)(2,1)} async-done(((bf16[1088,3264]{1,0:T(8,128)(2,1)}), bf16[272,3264]{1,0:T(8,128)(2,1)}) %reduce-scatter.7.cloned.1.call-update) | async-done | bytes 1775632 | tf_op jit(solution)/shard_map/reduce_scatter | solution.py:282
  556.7 84.9 %reduce-scatter.13.cloned.1.call-done = bf16[1088,1088]{1,0:T(8,128)(2,1)} async-done(((bf16[4352,1088]{1,0:T(8,128)(2,1)}), bf16[1088,1088]{1,0:T(8,128)(2,1)}) %reduce-scatter.13.cloned.1.call-update) | async-done | bytes 2367504
  645.7 80.6 %reduce-scatter.11.cloned.1.call-done = bf16[1088,1088]{1,0:T(8,128)(2,1)} async-done(((bf16[4352,1088]{1,0:T(8,128)(2,1)}), bf16[1088,1088]{1,0:T(8,128)(2,1)}) %reduce-scatter.11.cloned.1.call-update) | async-done | bytes 2367504 | tf_op jit(solution)/shard_map/reduce_scatter | solution.py:306
  726.4 573.8 %all-reduce.21 = (f32[272]{0:T(512)}, f32[272]{0:T(512)}, f32[272,3264]{1,0:T(8,128)}, f32[544]{0:T(1024)}, f32[272,1088]{1,0:T(8,128)}, /*index=5*/f32[272]{0:T...) all-reduce(f32[272]{0:T(512)S(1)} %get-tuple-element.178, ...), channel_id=1, replica_groups=mesh['ctx'=8,'wsh'=4] {'ctx'}, use_global_device_ids=true, to_apply=%region_16.17 | all-reduce | flops 3554499 | bytes 21333528 | tf_op jit(solution)/shard_map/psum | solution.py:313
  (230 shorter events, 87.3 us)
Async XLA Ops:
  7.2 25.8 %copy-start.2 = (bf16[1,128,1088]{1,2,0:T(8,128)(2,1)S(1)}, bf16[1,128,1088]{1,2,0:T(8,128)(2,1)}, u32[]{:S(2)}) copy-start(bf16[1,128,1088]{1,2,0:T(8,128)(2,1)} %param.17) | copy-start | bytes 835588
  7.2 57.8 %all-gather.11.cloned.1.call-start = ((), (), s32[]{:S(2)}) async-start(), calls=%async_computation.4 | async-start | bytes 9052160 | tf_op jit(solution)/shard_map/all_gather | solution.py:106
  7.9 165.1 %all-gather.15.cloned.1.call-start = ((), (), s32[]{:S(2)}) async-start(), calls=%async_computation.6 | async-start | bytes 2506752 | tf_op jit(solution)/shard_map/all_gather | solution.py:134
  33.2 38.2 %copy-start.17 = (f32[128]{0:T(128)}, f32[128]{0:T(128)S(1)}, u32[]{:S(2)}) copy-start(f32[128]{0:T(128)S(1)} %broadcast_multiply_fusion.1) | copy-start | bytes 1540
  33.3 38.1 %copy-start.37 = (f32[128]{0:T(128)}, f32[128]{0:T(128)S(1)}, u32[]{:S(2)}) copy-start(f32[128]{0:T(128)S(1)} %fusion.70) | copy-start | bytes 1540
  33.4 38.0 %copy-start.21 = (f32[128]{0:T(128)}, f32[128]{0:T(128)S(1)}, u32[]{:S(2)}) copy-start(f32[128]{0:T(128)S(1)} %fusion.83) | copy-start | bytes 1540
  72.3 109.8 %all-gather.13.cloned.1.call-start = ((), (), s32[]{:S(2)}) async-start(), calls=%async_computation.5 | async-start | bytes 2506752 | tf_op jit(solution)/shard_map/all_gather | solution.py:135
  73.1 132.9 %all-gather.17.cloned.1.call-start = ((), (), s32[]{:S(2)}) async-start(), calls=%async_computation.7 | async-start | bytes 3133440 | tf_op jit(solution)/shard_map/all_gather | solution.py:108
  73.7 201.9 %all-gather.19.cloned.1.call-start = ((), (), s32[]{:S(2)}) async-start(), calls=%async_computation.8 | async-start | bytes 12533760 | tf_op jit(solution)/shard_map/all_gather | solution.py:112
  77.0 96.1 %copy-start.7 = (bf16[128,1088]{0,1:T(8,128)(2,1)S(1)}, bf16[128,1088]{0,1:T(8,128)(2,1)}, u32[]{:S(2)}) copy-start(bf16[128,1088]{0,1:T(8,128)(2,1)} %get-tuple-element.156) | copy-start | bytes 835588
  77.0 267.6 %all-gather.21.cloned.1.call-start = ((), (), s32[]{:S(2)}) async-start(), calls=%async_computation.9 | async-start | bytes 12533760 | tf_op jit(solution)/shard_map/all_gather | solution.py:114
  77.6 352.4 %all-gather.23.cloned.1.call-start = ((), (), s32[]{:S(2)}) async-start(), calls=%async_computation.10 | async-start | bytes 2506752 | tf_op jit(solution)/shard_map/all_gather | solution.py:210
  102.0 71.0 %copy-start.28 = (s32[128]{0:T(128)}, s32[128]{0:T(128)S(1)}, u32[]{:S(2)}) copy-start(s32[128]{0:T(128)S(1)} %get-tuple-element.153) | copy-start | bytes 1540
  102.1 6.4 collective-permute-start
  108.4 6.3 collective-permute-start.1
  114.7 6.3 collective-permute-start.2
  114.7 62.1 %copy-start.32 = (s32[128]{0:T(128)}, s32[128]{0:T(128)S(1)}, u32[]{:S(2)}) copy-start(s32[128]{0:T(128)S(1)} %iota_add_fusion) | copy-start | bytes 1540
  121.1 32.4 %collective-permute-start.3 = (s32[128]{0:T(128)S(1)}, s32[128]{0:T(128)S(1)}, u32[]{:S(2)}, u32[]{:S(2)}) collective-permute-start(s32[128]{0:T(128)S(1)} %collective-permute-done.2), channel_id=1, source_target_pairs={{0,4},{4,8},{8,12},{12,16},{16,20},{20,24},{24,28},{28,0},{1,5},{5... | collective-permute-start | bytes 1544 | tf_op jit(solution)/shard_map/ppermute | solution.py:138
  153.4 6.2 collective-permute-start.4
  159.7 6.2 collective-permute-start.5
  165.9 6.2 collective-permute-start.6
  172.8 280.3 %all-gather.25.cloned.1.call-start = ((), (), s32[]{:S(2)}) async-start(), calls=%async_computation.11 | async-start | bytes 2506752 | tf_op jit(solution)/shard_map/all_gather | solution.py:213
  189.0 22.0 %copy-start.14 = (bf16[128,17,64]{0,2,1:T(8,128)(2,1)}, bf16[128,17,64]{0,2,1:T(8,128)(2,1)S(1)}, u32[]{:S(2)}) copy-start(bf16[128,17,64]{0,2,1:T(8,128)(2,1)S(1)} %get-tuple-element.168) | copy-start | bytes 835588
  210.9 133.7 %copy-start.6 = (bf16[1,128,1088]{1,2,0:T(8,128)(2,1)S(1)}, bf16[1,128,1088]{1,2,0:T(8,128)(2,1)}, u32[]{:S(2)}) copy-start(bf16[1,128,1088]{1,2,0:T(8,128)(2,1)} %param.31) | copy-start | bytes 835588
  369.4 160.5 %reduce-scatter.9.cloned.1.call-start = ((), (), s32[]{:S(2)}) async-start(), calls=%async_computation.13 | async-start | bytes 3133440 | tf_op jit(solution)/shard_map/reduce_scatter | solution.py:288
  372.8 183.9 %reduce-scatter.7.cloned.1.call-start = ((), (), s32[]{:S(2)}) async-start(), calls=%async_computation.12 | async-start | bytes 9052160 | tf_op jit(solution)/shard_map/reduce_scatter | solution.py:282
  446.0 13.8 %copy-start.16 = (pred[1024,128]{0,1:T(8,128)(4,1)S(1)}, pred[1024,128]{0,1:T(8,128)(4,1)}, u32[]{:S(2)}) copy-start(pred[1024,128]{0,1:T(8,128)(4,1)} %fusion.74) | copy-start | bytes 393220
  476.9 164.7 %reduce-scatter.13.cloned.1.call-start = ((), (), s32[]{:S(2)}) async-start(), calls=%async_computation.15 | async-start | bytes 12533760
  498.3 228.1 %reduce-scatter.11.cloned.1.call-start = ((), (), s32[]{:S(2)}) async-start(), calls=%async_computation.14 | async-start | bytes 12533760 | tf_op jit(solution)/shard_map/reduce_scatter | solution.py:306
  509.5 19.4 %copy-start.4 = (f32[128,1088]{0,1:T(8,128)S(1)}, f32[128,1088]{0,1:T(8,128)}, u32[]{:S(2)}) copy-start(f32[128,1088]{0,1:T(8,128)} %copy-done.3) | copy-start | bytes 1671172
  509.5 19.4 %copy-start.35 = (f32[128]{0:T(128)S(1)}, f32[128]{0:T(128)}, u32[]{:S(2)}) copy-start(f32[128]{0:T(128)} %copy-done.34) | copy-start | bytes 1540
  641.6 84.8 %copy-start.15 = (bf16[272,1088]{1,0:T(8,128)(2,1)S(1)}, bf16[272,1088]{1,0:T(8,128)(2,1)}, u32[]{:S(2)}) copy-start(bf16[272,1088]{1,0:T(8,128)(2,1)} %reduce-scatter.9.cloned.1.call-done) | copy-start | bytes 1775620
  (29 other events, 123.8 us)
Sparse Core Ops, SparseCore 0:
  9.6 55.3 all-gather.10
  72.5 54.2 all-gather.14
  128.8 52.5 all-gather.12
  182.8 23.0 all-gather.16
  207.9 67.5 all-gather.18
  277.0 67.5 all-gather.20
  347.2 53.1 all-gather.22
  402.4 50.6 all-gather.24
  456.3 32.1 reduce-scatter.8
  491.1 65.5 reduce-scatter.6
  559.3 82.2 reduce-scatter.12
  644.1 82.2 reduce-scatter.10
